TPU v7x, 32 devices: a whole 2x2x4 slice. The times are simulated.
32 devices in a mesh: mol: 8 (over z, core), stream: 2 (over y), head: 2 (over x).
Axes of the slice: x: 2, y: 2, z: 4, core: 2. Of those that a mesh axis runs over, the one named last changes fastest.
Arguments:
- tokens: bfloat16 [8192, 768], P(('mol', 'stream')), may hold values from -6 to 6
- cotangent: float32 [8192, 768], P(('mol', 'stream')), may hold values from -6 to 6
- attn_gain: float32 [768], replicated, may hold values from 0.25 to 1.75
- attn_shift: float32 [768], replicated, may hold values from -2 to 2
- query_weight: bfloat16 [768, 768], P(None, 'head'), may hold values from -0.21875 to 0.21875
- query_bias: float32 [768], P('head'), may hold values from -3 to 3
- key_weight: bfloat16 [768, 768], P(None, 'head'), may hold values from -0.21875 to 0.21875
- value_weight: bfloat16 [768, 768], P(None, 'head'), may hold values from -0.21875 to 0.21875
- value_bias: float32 [768], P('head'), may hold values from -3 to 3
- out_weight: bfloat16 [768, 768], P('head'), may hold values from -0.875 to 0.875
- out_bias: float32 [768], replicated, may hold values from -3 to 3
- ffn_gain: float32 [768], replicated, may hold values from 0.25 to 1.75
- ffn_shift: float32 [768], replicated, may hold values from -2 to 2
- up_weight: bfloat16 [768, 768], P(None, 'head'), may hold values from -0.21875 to 0.21875
- up_bias: bfloat16 [768], P('head'), may hold values from -3 to 3
- down_weight: bfloat16 [768, 768], P('head'), may hold values from -0.3125 to 0.3125
- down_bias: float32 [768], replicated, may hold values from -3 to 3
- atom_counts: int32 [8, 16], P('mol'), may hold values from 1 to 24, 154 in all within a row
- edge_counts: int32 [8, 16], P('mol'), may hold values from 1 to 64, 512 in all within a row
Outputs:
- output: float32 [8192, 768], P(('mol', 'stream'))
- tokens_grad: float32 [8192, 768], P(('mol', 'stream'))
- attn_gain_grad: float32 [768], P('head')
- attn_shift_grad: float32 [768], P('head')
- query_weight_grad: float32 [768, 768], P(None, 'head')
- query_bias_grad: float32 [768], P('head')
- key_weight_grad: float32 [768, 768], P(None, 'head')
- value_weight_grad: float32 [768, 768], P(None, 'head')
- value_bias_grad: float32 [768], P('head')
- out_weight_grad: float32 [768, 768], P('head')
- out_bias_grad: float32 [768], P('head')
- ffn_gain_grad: float32 [768], P('head')
- ffn_shift_grad: float32 [768], P('head')
- up_weight_grad: float32 [768, 768], P(None, 'head')
- up_bias_grad: float32 [768], P('head')
- down_weight_grad: float32 [768, 768], P('head')
- down_bias_grad: float32 [768], P('head')
Inputs may be any that keep to these rules, and one draw needn't show every extreme that they name: `atom_counts`: A row holds the atom counts of the 16 molecules of one mol index; each row sums to exactly 154, and its largest entry is exactly 24. `edge_counts`: A row holds the edge token counts of the 16 molecules of one mol index; each row sums to exactly 512, and its largest entry is exactly 64.
All inputs are finite; a program needn't handle non-finite values.
Results may differ from a plain program's by a relative error of at most 0.013.
Values may be sent and summed in bfloat16 or wider, within the bound.
A program may use at most 256 MiB of HBM per device.

v0:
```python
import functools
import math

import jax
import jax.numpy as jnp
from jax import lax
from jax.experimental import pallas as pl
from jax.experimental.pallas import tpu as pltpu
from jax.sharding import PartitionSpec as P

HEAD_DIM = 24
BF = jnp.bfloat16
F32 = jnp.float32
MESH = pl.DeviceIdType.MESH
EDGES = 512
NODES = 192
TOTAL = EDGES + NODES
PADDED = 768
HEADS_HERE = 8
SCALE = HEAD_DIM ** (-0.5)
SCALE2 = SCALE * math.log2(math.e)
BLOCKS = (
    (0, 128, ((0, 256), (512, 256))),
    (128, 128, ((64, 256), (512, 256))),
    (256, 128, ((192, 256), (512, 256))),
    (384, 128, ((256, 256), (512, 256))),
    (512, 192, ((0, 768),)),
)
OWNERS = (((0, 0), 512, 192), ((1, 0), 0, 256), ((1, 1), 256, 256))


def nn(a, b):
    return jnp.dot(a, b, preferred_element_type=F32)


def nt(a, b):
    return lax.dot_general(a, b, (((1,), (1,)), ((), ())), preferred_element_type=F32)


def tn(a, b):
    return lax.dot_general(a, b, (((0,), (0,)), ((), ())), preferred_element_type=F32)


def row_loop(count, step, fn, init):
    def body(i, carry):
        return fn(pl.ds(pl.multiple_of(i * step, step), step), carry)

    return lax.fori_loop(0, count // step, body, init)


def normed(x):
    mu = jnp.mean(x, axis=-1, keepdims=True)
    xc = x - mu
    var = jnp.mean(xc * xc, axis=-1, keepdims=True)
    r = lax.rsqrt(var + 1e-05)
    return xc * r, r


def col_sum(x):
    return jnp.sum(x, axis=0, keepdims=True)


SEM = {}


def sem_id(name, count=1):
    if name not in SEM:
        SEM[name] = sum(n for _, n in SEM.values()), count
    return SEM[name][0]


N_SEMS = 160
N_LOCAL = 24


def layer_kernel(
    tokens, cot, wq, wk, wv, wo, wu, wd,
    atoms, edges,
    a_gain_v, a_shift_v, q_bias_v, v_bias_v, o_bias_v, f_gain_v, f_shift_v, u_bias_v, d_bias_v,
    d_out, d_tok, f1, f2, vec,
    dov, dtv, zb, fz1, fz2, dxp, tok, res, cotv, ww, fwo, fwu, fwd, ub, fin1, qkv, dxw, qm, dam,
    p0, p1, p2, p3, p4, bias, segc, attf, att, ain, da, delta,
    t0, t1, n2s, r2s, mid, sec, hid, dc, ig, ac, ato, ago, mgd,
    ds, dkf, dvf,
    g1, gs1, xr, gx, yr, gq, zr1, g2, gs2, zr2, fp, fx, fs, fy,
    va, vq, vz, vc,
    ss, rs, ls,
):
    m, s, h = lax.axis_index("mol"), lax.axis_index("stream"), lax.axis_index("head")
    z, c = m // 2, lax.rem(m, 2)
    zc = lax.axis_size("mol") // 2
    me = 2 * s + h
    x_peer, y_peer, xy_peer = (m, s, 1 - h), (m, 1 - s, h), (m, 1 - s, 1 - h)
    quad = (x_peer, y_peer, xy_peer)
    twin = (2 * z + 1 - c, s, h)
    z_peers = [(2 * lax.rem(z + d, zc) + c, s, h) for d in range(1, zc)]

    def remote(name, src, dst, dev, k=0, count=1):
        i = sem_id(name, count) + k
        return pltpu.make_async_remote_copy(
            src_ref=src, dst_ref=dst, send_sem=ss.at[i], recv_sem=rs.at[i],
            device_id=dev, device_id_type=MESH,
        )

    def as_row(ref):
        return ref[...].astype(F32).reshape(1, -1)

    a_gain, a_shift, f_gain, f_shift = (as_row(r) for r in (a_gain_v, a_shift_v, f_gain_v, f_shift_v))
    o_bias, d_bias, q_bias, v_bias = (as_row(r) for r in (o_bias_v, d_bias_v, q_bias_v, v_bias_v))

    def local(k, src, dst):
        return pltpu.make_async_copy(src, dst, ls.at[k])

    own = pl.multiple_of(256 * h, 256)
    other = pl.multiple_of(256 * (1 - h), 256)
    window = pl.multiple_of(128 * s, 128)

    loads = [
        local(0, tokens.at[pl.ds(own, 256)], res),
        local(1, cot.at[pl.ds(own, 256)], cotv),
        local(2, wq.at[:, pl.ds(window, 256)], ww.at[:, 0:256]),
        local(3, wk.at[:, pl.ds(window, 256)], ww.at[:, 256:512]),
        local(4, wv.at[:, pl.ds(window, 256)], ww.at[:, 512:768]),
        local(5, wo, fwo.at[h]),
        local(6, wu, fwu.at[h]),
        local(7, wd, fwd.at[h]),
    ]
    edge_load = local(8, tokens, tok.at[0:EDGES])
    node_load = local(9, tokens.at[0:NODES], tok.at[EDGES:TOTAL])
    pl.when(s == 1)(edge_load.start)
    pl.when(s == 0)(node_load.start)
    for copy in loads:
        copy.start()
    ub[h] = jnp.broadcast_to(as_row(u_bias_v), (8, 384))

    barrier = pltpu.get_barrier_semaphore()
    greeted = [*quad, twin, *z_peers]
    for dev in greeted:
        pl.semaphore_signal(barrier, inc=1, device_id=dev, device_id_type=MESH)
    pl.semaphore_wait(barrier, len(greeted))

    def edge_part(k, half):
        rows = pl.ds(pl.multiple_of(256 * half + 64 * k, 64), 64)
        return rows

    tok_y = [
        remote("tok_y", tokens.at[edge_part(k, h)], tok.at[edge_part(k, h)], y_peer, k, 4)
        for k in range(4)
    ]
    tok_x = [
        remote("tok_x", tok.at[edge_part(k, h)], tok.at[edge_part(k, h)], x_peer, k, 4)
        for k in range(4)
    ]
    tok_x_in = [
        remote("tok_x", tok.at[edge_part(k, 1 - h)], tok.at[edge_part(k, 1 - h)], x_peer, k, 4)
        for k in range(4)
    ]
    tok_n = remote("tok_n", tokens.at[0:NODES], tok.at[EDGES:TOTAL], y_peer)

    @pl.when(s == 1)
    def _():
        for copy in tok_y:
            copy.start()

    pl.when(s == 0)(tok_n.start)
    u_send = remote("ub", ub.at[h], ub.at[h], x_peer)
    u_send.start()
    part_o = pl.ds(pl.multiple_of(192 * c, 192), 192)
    part_u = pl.ds(pl.multiple_of(384 * c, 384), 384)
    w_out = [
        remote("wo_x", wo.at[part_o], fwo.at[h, part_o], x_peer),
        remote("wu_x", wu.at[part_u], fwu.at[h, part_u], x_peer),
        remote("wd_x", wd.at[part_o], fwd.at[h, part_o], x_peer),
    ]

    @pl.when(s == 1)
    def _():
        for k in (0, 2, 1):
            w_out[k].start()

    w_in = [
        remote("wo_x", wo.at[part_o], fwo.at[1 - h, part_o], x_peer),
        remote("wu_x", wu.at[part_u], fwu.at[1 - h, part_u], x_peer),
        remote("wd_x", wd.at[part_o], fwd.at[1 - h, part_o], x_peer),
    ]
    w_twin = [
        remote("wo_c", fwo.at[1 - h, part_o], fwo.at[1 - h, part_o], twin),
        remote("wu_c", fwu.at[1 - h, part_u], fwu.at[1 - h, part_u], twin),
        remote("wd_c", fwd.at[1 - h, part_o], fwd.at[1 - h, part_o], twin),
    ]

    w_y = {
        0: remote("wo_y", fwo.at[1 - h, part_o], fwo.at[1 - h, part_o], y_peer),
        2: remote("wd_y", fwd.at[1 - h, part_o], fwd.at[1 - h, part_o], y_peer),
    }

    def pass_weight(k):
        w_in[k].wait_recv()
        w_y[k].start()
        w_twin[k].start()

    def share_weight(k):
        w_in[k].wait_recv()
        w_twin[k].start()

    def take_weight(k):
        w_y[k].wait_recv()
        w_twin[k].start()

    def ends_of(counts, added):
        total, ends = 0, []
        for j in range(counts.shape[1]):
            total = total + counts[0, j] + added
            ends.append(total)
        return ends

    node_ends, edge_ends = ends_of(atoms, 1), ends_of(edges, 0)
    live_count = jnp.where(s == 0, node_ends[-1], edge_ends[-1])

    def seg_of(position, ends):
        seg = jnp.zeros_like(position)
        for end in ends:
            seg = seg + jnp.where(position >= end, 1, 0)
        return seg

    segc[0:EDGES] = seg_of(lax.broadcasted_iota(jnp.int32, (EDGES, 1), 0), edge_ends)
    segc[EDGES:TOTAL] = seg_of(lax.broadcasted_iota(jnp.int32, (NODES, 1), 0), node_ends)
    at_row = lax.broadcasted_iota(jnp.int32, (1, PADDED), 1)
    seg_r = jnp.where(at_row < EDGES, seg_of(at_row, edge_ends), seg_of(at_row - EDGES, node_ends))
    seg_r = jnp.where(at_row < TOTAL, seg_r, -1)

    lane = lax.broadcasted_iota(jnp.int32, (1, 256), 1) - 64 * s
    head_of = jnp.where((lane >= 0) & (lane < 192), lane // HEAD_DIM, -1)
    zero = jnp.zeros((), BF)

    qkv[TOTAL:PADDED] = jnp.zeros((PADDED - TOTAL, 768), BF)
    bias_row = jnp.concatenate(
        [
            jnp.where(s == 0, q_bias[:, 0:256], q_bias[:, 128:384]),
            jnp.zeros((1, 256), F32),
            jnp.where(s == 0, v_bias[:, 0:256], v_bias[:, 128:384]),
        ],
        axis=1,
    )

    def project(first, count):
        def norm_rows(i, carry):
            rows = pl.ds(pl.multiple_of(first + i * 64, 64), 64)
            n1, _ = normed(tok[rows].astype(F32))
            fin1[rows] = (n1 * a_gain + a_shift).astype(BF)
            return carry

        lax.fori_loop(0, count // 64, norm_rows, 0)
        rows = pl.ds(pl.multiple_of(first, 64), count)
        qkv[rows] = (nn(fin1[rows], ww[...]) + bias_row).astype(BF)

    for copy in loads[2:5]:
        copy.wait()

    @pl.when(s == 1)
    def _():
        edge_load.wait()
        project(0, EDGES)
        tok_n.wait_recv()
        project(EDGES, NODES)
        pass_weight(0)

    @pl.when(s == 0)
    def _():
        node_load.wait()
        project(EDGES, NODES)
        for k in range(4):
            tok_y[k].wait_recv()
            tok_x[k].start()
        w_out[1].start()
        project(own, 256)
        for k in range(4):
            tok_x_in[k].wait_recv()
        project(other, 256)

    for j in range(HEADS_HERE):
        qm[j] = jnp.where(head_of == j, qkv[0:TOTAL, 0:256], zero)

    def send_rows(name, src, dst, k):
        dev_sh, first, count = OWNERS[k]
        target = (m, *dev_sh)
        mine = 2 * dev_sh[0] + dev_sh[1]

        @pl.when(me != mine)
        def _():
            i = sem_id(name + "_s", 3) + k
            j = sem_id(name, 4) + me
            pltpu.make_async_remote_copy(
                src_ref=src.at[first:first + count], dst_ref=dst.at[me, 0:count],
                send_sem=ss.at[i], recv_sem=rs.at[j], device_id=target, device_id_type=MESH,
            ).start()

        @pl.when(me == mine)
        def _():
            dst[mine, 0:count] = src[first:first + count]

    def wait_rows(name, src, dst):
        for k, (dev_sh, first, count) in enumerate(OWNERS):
            mine = 2 * dev_sh[0] + dev_sh[1]

            @pl.when(me == mine)
            def _():
                for r in range(4):
                    if r != mine:
                        j = sem_id(name, 4) + r
                        pltpu.make_async_remote_copy(
                            src_ref=src.at[first:first + count], dst_ref=dst.at[r, 0:count],
                            send_sem=ss.at[j], recv_sem=rs.at[j], device_id=x_peer, device_id_type=MESH,
                        ).wait_recv()

    def wait_sent(name, src, dst):
        for k, (dev_sh, first, count) in enumerate(OWNERS):
            mine = 2 * dev_sh[0] + dev_sh[1]

            @pl.when(me != mine)
            def _():
                i = sem_id(name + "_s", 3) + k
                pltpu.make_async_remote_copy(
                    src_ref=src.at[first:first + count], dst_ref=dst.at[me, 0:count],
                    send_sem=ss.at[i], recv_sem=rs.at[i], device_id=(m, *dev_sh), device_id_type=MESH,
                ).wait_send()

    def pick_heads(stacked, rows):
        total = None
        for j in range(HEADS_HERE):
            part = jnp.where(head_of == j, stacked[j * rows:(j + 1) * rows], 0.0)
            total = part if total is None else total + part
        return total

    probs = (p0, p1, p2, p3, p4)
    to_owner = (None, 1, None, 2, 0)
    group = 4

    @pl.when(s == 0)
    def _():
        ain[:, NODES:256] = jnp.zeros((4, 256 - NODES, 256), BF)

    @pl.when((s == 0) & (h == 1))
    def _():
        ain[:, 0:NODES] = jnp.zeros((4, NODES, 256), BF)

    for b, (q0, qn, segs) in enumerate(BLOCKS):
        o = 0
        for a, n in segs:
            bias[0:qn, o:o + n] = jnp.where(segc[q0:q0 + qn] == seg_r[:, a:a + n], 0.0, -1e30)
            o += n
        for j0 in range(0, HEADS_HERE, group):
            qb = qm[j0:j0 + group, q0:q0 + qn, :].reshape(group * qn, 256)
            raw = [nt(qb, qkv[a:a + n, 256:512]) for a, n in segs]
            for g in range(group):
                j, o, parts = j0 + g, 0, []
                for piece, (a, n) in zip(raw, segs):
                    parts.append(piece[g * qn:(g + 1) * qn] * SCALE2 + bias[0:qn, o:o + n])
                    o += n
                top = functools.reduce(
                    jnp.maximum, [jnp.max(x, axis=1, keepdims=True) for x in parts]
                )
                parts = [jnp.exp2(x - top) for x in parts]
                inv = 1.0 / sum(jnp.sum(x, axis=1, keepdims=True) for x in parts)
                o = 0
                for x, (a, n) in zip(parts, segs):
                    probs[b][j * qn:(j + 1) * qn, o:o + n] = (x * inv).astype(BF)
                    o += n
        o, acc = 0, None
        for a, n in segs:
            part = nn(probs[b][:, o:o + n], qkv[a:a + n, 512:768])
            acc = part if acc is None else acc + part
            o += n
        picked = pick_heads(acc, qn)
        attf[q0:q0 + qn] = picked
        att[q0:q0 + qn] = picked.astype(BF)
        if to_owner[b] is not None:
            send_rows("att", att, ain, to_owner[b])

    @pl.when(s == 1)
    def _():
        pass_weight(2)

    @pl.when(s == 0)
    def _():
        take_weight(0)

    share_weight(1)

    cut = [slice(0, 384), slice(384, 768)]
    g1_of = (
        lambda cc, xh: tn(hid[:, cut[xh]], dc[:, cut[cc]]),
        lambda cc, xh: tn(sec[:, cut[cc]], ig[:, cut[xh]]),
        lambda cc, xh: tn(ato[:, cut[xh]], ac[:, cut[cc]]),
    )
    g1_twin = [remote("g1_c", g1.at[p, 1 - c], gs1.at[p], twin, p, 3) for p in range(3)]

    def g1_compute(p):
        for cc in range(2):
            for xh in range(2):
                g1[p, cc, xh] = g1_of[p](cc, xh).astype(BF)
        g1_twin[p].start()

    rows_y = pl.ds(pl.multiple_of(192 * (1 - s), 192), 192)
    rows_s = pl.ds(pl.multiple_of(192 * s, 192), 192)
    y_first = (True, True, False)
    g1_x = [
        remote("g1_x", gx.at[p, 1 - h, 0:192], xr.at[p, 0:192], x_peer, p, 3)
        if y_first[p] else remote("g1_x", gs1.at[p, 1 - h], xr.at[p], x_peer, p, 3)
        for p in range(3)
    ]
    g1_y = [
        remote("g1_y", gs1.at[p, :, rows_y], yr.at[p], y_peer, p, 3)
        if y_first[p] else remote("g1_y", gx.at[p, 0, rows_y], yr.at[p, 0], y_peer, p, 3)
        for p in range(3)
    ]
    zn1, zn2 = 192 // zc, 384 // zc

    def chunk(t, n):
        return pl.ds(pl.multiple_of(n * t, n), n)

    g1_z = [
        [
            remote("g1_z", gq.at[p, chunk(lax.rem(z + d, zc), zn1)], zr1.at[p, d - 1], z_peers[d - 1],
                   p * (zc - 1) + d - 1, 3 * (zc - 1))
            for d in range(1, zc)
        ]
        for p in range(3)
    ]

    def add_into(dst, *terms):
        x = terms[0].astype(F32)
        for t in terms[1:]:
            x = x + t.astype(F32)
        dst[...] = x.astype(BF)

    def g1_after_twin(p):
        g1_twin[p].wait_recv()
        for xh in range(2):
            add_into(gs1.at[p, xh], g1[p, c, xh], gs1[p, xh])
        (g1_y if y_first[p] else g1_x)[p].start()

    def g1_after_x(p):
        g1_x[p].wait_recv()
        if y_first[p]:
            add_into(gq.at[p], gx[p, h, 0:192], xr[p, 0:192])
            for copy in g1_z[p]:
                copy.start()
        else:
            add_into(gx.at[p, 0], gs1[p, h], xr[p])
            g1_y[p].start()

    def g1_after_y(p):
        g1_y[p].wait_recv()
        if y_first[p]:
            for xh in range(2):
                add_into(gx.at[p, xh, 0:192], gs1[p, xh, rows_s], yr[p, xh])
            g1_x[p].start()
        else:
            add_into(gq.at[p], gx[p, 0, rows_s], yr[p, 0])
            for copy in g1_z[p]:
                copy.start()

    for copy in (loads[0], loads[1], *loads[5:8]):
        copy.wait()
    row_at = lax.broadcasted_iota(jnp.int32, (256, 1), 0) + own
    live_all = jnp.where(row_at < live_count, 1.0, 0.0)
    r2s[:, 1:2] = live_all
    wait_rows("att", att, ain)
    for x in range(2):
        ato[:, 384 * x:384 * x + 128] = ain[x, :, 0:128]
        ato[:, 384 * x + 128:384 * x + 256] = ain[x, :, 128:256] + ain[2 + x, :, 0:128]
        ato[:, 384 * x + 256:384 * x + 384] = ain[2 + x, :, 128:256]
    twin_o = pl.ds(pl.multiple_of(192 * (1 - c), 192), 192)
    twin_u = pl.ds(pl.multiple_of(384 * (1 - c), 384), 384)
    w_twin_in = [
        remote("wo_c", fwo.at[1 - h, twin_o], fwo.at[1 - h, twin_o], twin),
        remote("wu_c", fwu.at[1 - h, twin_u], fwu.at[1 - h, twin_u], twin),
        remote("wd_c", fwd.at[1 - h, twin_o], fwd.at[1 - h, twin_o], twin),
    ]
    w_twin_in[0].wait_recv()
    wo_all = fwo[...].reshape(768, 768)
    t0[...] = nn(ato[...], wo_all)
    pl.when(s == 0)(lambda: take_weight(2))
    live_of = lambda rows: r2s[rows, 1:2]

    def middle_rows(rows, carry):
        x = res[rows].astype(F32) + live_of(rows) * (t0[rows] + o_bias)
        mid[rows] = x
        n2, r2 = normed(x)
        n2s[rows] = n2
        r2s[rows, 0:1] = r2
        sec[rows] = (n2 * f_gain + f_shift).astype(BF)
        return carry

    row_loop(256, 64, middle_rows, 0)
    w_twin_in[1].wait_recv()
    u_recv = remote("ub", ub.at[1 - h], ub.at[1 - h], x_peer)
    u_recv.wait_recv()
    for x in range(2):
        t0[:, 384 * x:384 * (x + 1)] = nn(sec[...], fwu[x]) + ub[x, 0:1]

    def gelu_rows(rows, carry):
        u = t0[rows]
        cdf = 0.5 * (1.0 + lax.erf(u * math.sqrt(0.5)))
        hid[rows] = (u * cdf).astype(BF)
        t1[rows] = cdf + u * (jnp.exp(-0.5 * u * u) * (1.0 / math.sqrt(2.0 * math.pi)))
        return carry

    row_loop(256, 64, gelu_rows, 0)
    w_twin_in[2].wait_recv()
    wd_all = fwd[...].reshape(768, 768)
    t0[...] = nn(hid[...], wd_all)
    zero_row = jnp.zeros((1, 768), F32)

    def out_rows(rows, carry):
        live = live_of(rows)
        x = (mid[rows] + live * (t0[rows] + d_bias)) - res[rows].astype(F32)
        dov[rows] = x.astype(BF)
        down = (live * cotv[rows]).astype(BF)
        dc[rows] = down
        return carry + col_sum(down.astype(F32))

    down_bias_sum = row_loop(256, 64, out_rows, zero_row)
    own_rows = pl.ds(own, 256)
    other_rows = pl.ds(other, 256)
    out_send = remote("out", dov, d_out.at[own_rows], x_peer)
    out_node = remote("out", dov.at[0:NODES], d_out.at[0:NODES], x_peer)
    pl.when(s == 1)(out_send.start)
    pl.when(me == 0)(out_node.start)
    g1_compute(0)
    stores = [local(10, dov, d_out.at[own_rows])]
    stores[0].start()
    zb[...] = jnp.zeros_like(zb)
    far = [local(18 + k, zb, ref.at[256:512]) for k, ref in enumerate((d_out, d_tok))]
    near = [local(18 + k, zb.at[NODES:256], ref.at[NODES:256]) for k, ref in enumerate((d_out, d_tok))]

    @pl.when(me == 0)
    def _():
        for copy in far:
            copy.start()

    @pl.when(me == 1)
    def _():
        for copy in near:
            copy.start()

    t0[...] = nt(dc[...], wd_all)

    def inner_rows(rows, carry):
        x = (t0[rows] * t1[rows]).astype(BF)
        ig[rows] = x
        return carry + col_sum(x.astype(F32))

    up_bias_sum = row_loop(256, 64, inner_rows, zero_row)
    g1_after_twin(0)
    t0[...] = nt(ig[:, 0:384], fwu[0]) + nt(ig[:, 384:768], fwu[1])

    def second_rows(rows, carry):
        gain_sum, shift_sum, bias_sum = carry
        sg, n2 = t0[rows], n2s[rows]
        g = sg * f_gain
        back = r2s[rows, 0:1] * (
            g - jnp.mean(g, axis=-1, keepdims=True) - n2 * jnp.mean(g * n2, axis=-1, keepdims=True)
        )
        mgd[rows] = back
        x = (live_of(rows) * (cotv[rows] + back)).astype(BF)
        ac[rows] = x
        return gain_sum + col_sum(sg * n2), shift_sum + col_sum(sg), bias_sum + col_sum(x.astype(F32))

    f_gain_sum, f_shift_sum, out_bias_sum = row_loop(
        256, 64, second_rows, (zero_row, zero_row, zero_row)
    )
    ago[...] = nt(ac[...], wo_all).astype(BF)

    for k, (dev_sh, first, count) in enumerate(OWNERS):
        mine = 2 * dev_sh[0] + dev_sh[1]

        @pl.when(me == mine)
        def _():
            for r in range(4):
                cols = slice(384 * (r % 2) + 128 * (r // 2), 384 * (r % 2) + 128 * (r // 2) + 256)
                if r == mine:
                    da[first:first + count] = ago[0:count, cols]
                else:
                    i, j = sem_id("da_s", 4) + r, sem_id("da", 3) + k
                    pltpu.make_async_remote_copy(
                        src_ref=ago.at[0:count, cols], dst_ref=da.at[first:first + count],
                        send_sem=ss.at[i], recv_sem=rs.at[j],
                        device_id=(m, r // 2, r % 2), device_id_type=MESH,
                    ).start()

    g1_compute(1)
    g1_compute(2)
    g1_after_twin(1)
    g1_after_twin(2)

    for k, (dev_sh, first, count) in enumerate(OWNERS):
        mine = 2 * dev_sh[0] + dev_sh[1]

        @pl.when(me != mine)
        def _():
            j = sem_id("da", 3) + k
            pltpu.make_async_remote_copy(
                src_ref=ago.at[0:count, 0:256], dst_ref=da.at[first:first + count],
                send_sem=ss.at[j], recv_sem=rs.at[j], device_id=x_peer, device_id_type=MESH,
            ).wait_recv()

    head_col = lax.broadcasted_iota(jnp.int32, (256, 128), 1)
    lane_row = lax.broadcasted_iota(jnp.int32, (256, 128), 0) - 64 * s
    head_pick = jnp.where(
        (lane_row >= 0) & (lane_row < 192) & (lane_row // HEAD_DIM == head_col), 1.0, 0.0
    ).astype(BF)
    prod = da[0:TOTAL].astype(F32) * attf[...]
    prod_hi = prod.astype(BF)
    delta[...] = nn(prod_hi, head_pick) + nn((prod - prod_hi.astype(F32)).astype(BF), head_pick)
    for j in range(HEADS_HERE):
        dam[j] = jnp.where(head_of == j, da[0:TOTAL], zero)
    dkf[...] = jnp.zeros_like(dkf)
    dvf[...] = jnp.zeros_like(dvf)
    for (q0, qn, segs), pr in zip(BLOCKS, probs):
        o = 0
        for a, n in segs:
            dv = None
            for j in range(HEADS_HERE):
                pv = tn(pr[j * qn:(j + 1) * qn, o:o + n], dam[j, q0:q0 + qn])
                dv = pv if dv is None else dv + pv
            dvf[a:a + n] += dv
            o += n
    dxw[:, 512:768] = dvf[0:TOTAL].astype(BF)

    lanes2 = [slice(0, 256), slice(256, 512), slice(512, 640)]
    g2_twin = [
        remote("g2_c", g2.at[1 - c, :, lanes2[p]], gs2.at[:, lanes2[p]], twin, p, 3) for p in range(3)
    ]
    g2_z = [
        [
            remote("g2_z", gs2.at[chunk(lax.rem(z + d, zc), zn2), lanes2[p]], zr2.at[d - 1, :, lanes2[p]],
                   z_peers[d - 1], p * (zc - 1) + d - 1, 3 * (zc - 1))
            for d in range(1, zc)
        ]
        for p in range(3)
    ]

    def tiles_of(k):
        first = dxw[:, 256 * k:256 * k + 128]
        last = dxw[:, 256 * k + 128:256 * k + 256]
        return jnp.where(s == 0, first, last), jnp.where(s == 0, last, first)

    def g2_compute(p):
        for cc in range(2):
            g2[cc, :, lanes2[p]] = tn(fin1[0:TOTAL, cut[cc]], dxp[:, lanes2[p]]).astype(BF)
        g2_twin[p].start()

    def g2_after_twin(p):
        g2_twin[p].wait_recv()
        add_into(gs2.at[:, lanes2[p]], g2[c, :, lanes2[p]], gs2[:, lanes2[p]])
        for copy in g2_z[p]:
            copy.start()

    stores.append(local(11, dtv, d_tok.at[own_rows]))
    st1, st2 = [None] * 3, [None] * 3
    f1_z, f1_y, f1_c, f2_z, f2_y, f2_c = [], [], [], [], [], []

    def f1_at(p, cc, ss_, zz):
        return f1.at[p, cc, pl.ds(pl.multiple_of(192 * ss_ + zn1 * zz, 16), zn1)]

    def f1_half(p, ss_):
        return f1.at[p, c, pl.ds(pl.multiple_of(192 * ss_, 192), 192)]

    def f2_at(p, cc, ss_, zz):
        return f2.at[ss_, pl.ds(pl.multiple_of(384 * cc + zn2 * zz, 16), zn2), lanes2[p]]

    def f2_half(p, ss_):
        return f2.at[ss_, pl.ds(pl.multiple_of(384 * c, 384), 384), lanes2[p]]

    def g1_after_z(p):
        for copy in g1_z[p]:
            copy.wait_recv()
        add_into(fz1.at[p], gq[p, chunk(z, zn1)], *[zr1[p, d] for d in range(zc - 1)])
        f1_z.append([
            remote("f1_z", fz1.at[p], f1_at(p, c, s, z), z_peers[d], p * (zc - 1) + d, 3 * (zc - 1))
            for d in range(zc - 1)
        ])
        for copy in f1_z[p]:
            copy.start()
        stores.append(local(12 + p, fz1.at[p], f1_at(p, c, s, z)))
        stores[-1].start()
        return stores[-1]

    def f1_after_z(p, store):
        for copy in f1_z[p]:
            copy.wait_recv()
        store.wait()
        f1_y.append(remote("f1_y", f1_half(p, s), f1_half(p, s), y_peer, p, 3))
        f1_c.append(remote("f1_c", f1_half(p, s), f1_half(p, s), twin, 2 * p, 6))
        f1_y[p].start()
        f1_c[-1].start()

    def f1_after_y(p):
        f1_y[p].wait_recv()
        f1_c.append(remote("f1_c", f1_half(p, 1 - s), f1_half(p, 1 - s), twin, 2 * p + 1, 6))
        f1_c[-1].start()

    def g2_after_z(p):
        for copy in g2_z[p]:
            copy.wait_recv()
        add_into(
            fz2.at[:, lanes2[p]], gs2[chunk(z, zn2), lanes2[p]], *[zr2[d, :, lanes2[p]] for d in range(zc - 1)]
        )
        f2_z.append([
            remote("f2_z", fz2.at[:, lanes2[p]], f2_at(p, c, s, z), z_peers[d], p * (zc - 1) + d, 3 * (zc - 1))
            for d in range(zc - 1)
        ])
        for copy in f2_z[p]:
            copy.start()
        stores.append(local(15 + p, fz2.at[:, lanes2[p]], f2_at(p, c, s, z)))
        stores[-1].start()
        return stores[-1]

    def f2_after_z(p, store):
        for copy in f2_z[p]:
            copy.wait_recv()
        store.wait()
        f2_y.append(remote("f2_y", f2_half(p, s), f2_half(p, s), y_peer, p, 3))
        f2_c.append(remote("f2_c", f2_half(p, s), f2_half(p, s), twin, 2 * p, 6))
        f2_y[p].start()
        f2_c[-1].start()

    def f2_after_y(p):
        f2_y[p].wait_recv()
        f2_c.append(remote("f2_c", f2_half(p, 1 - s), f2_half(p, 1 - s), twin, 2 * p + 1, 6))
        f2_c[-1].start()


    dxp[:, 0:128], dxp[:, 128:256] = tiles_of(2)
    g2_compute(0)
    g1_after_y(0)
    for b, (q0, qn, segs) in enumerate(BLOCKS):
        pr = probs[b]
        for j0 in range(0, HEADS_HERE, group):
            ab = dam[j0:j0 + group, q0:q0 + qn, :].reshape(group * qn, 256)
            o = 0
            for a, n in segs:
                pg = nt(ab, qkv[a:a + n, 512:768])
                for g in range(group):
                    j = j0 + g
                    r = slice(j * qn, (j + 1) * qn)
                    ds[r, o:o + n] = (
                        pr[r, o:o + n].astype(F32)
                        * (pg[g * qn:(g + 1) * qn] - delta[q0:q0 + qn, j:j + 1])
                    ).astype(BF)
                o += n
        o, acc = 0, None
        for a, n in segs:
            part = nn(ds[0:HEADS_HERE * qn, o:o + n], qkv[a:a + n, 256:512])
            acc = part if acc is None else acc + part
            o += n
        dxw[q0:q0 + qn, 0:256] = (pick_heads(acc, qn) * SCALE).astype(BF)
        o = 0
        for a, n in segs:
            dk = None
            for j in range(HEADS_HERE):
                pk = tn(ds[j * qn:(j + 1) * qn, o:o + n], qm[j, q0:q0 + qn])
                dk = pk if dk is None else dk + pk
            dkf[a:a + n] += dk
            o += n
        if b == 0:
            g2_after_twin(0)
        if b == 1:
            g1_after_x(0)
            g1_after_y(1)
        if b == 2:
            g1_after_x(2)
        if b == 3:
            g1_after_x(1)
            st2[0] = g2_after_z(0)
    dxw[:, 256:512] = (dkf[0:TOTAL] * SCALE).astype(BF)
    q_full, q_half = tiles_of(0)
    k_full, k_half = tiles_of(1)
    dxp[:, 256:384], dxp[:, 384:512] = q_full, k_full
    dxp[:, 512:640] = (q_half.astype(F32) + pltpu.roll(k_half.astype(F32), 64, 1)).astype(BF)

    fp_x = [
        remote("fp_x", fp.at[chunk(2 * (1 - h) + k, 128)], fx.at[chunk(k, 128)], x_peer, k, 3)
        for k in range(2)
    ]
    fp_xn = [
        remote("fp_xn", fs.at[256 + 96 * k:256 + 96 * (k + 1)], fx.at[256 + 96 * k:256 + 96 * (k + 1)], x_peer, k, 2)
        for k in range(2)
    ]
    fp_y = [
        remote("fp_y", fs.at[chunk(k, 128)], fy.at[chunk(k, 128)], y_peer, k, 2) for k in range(2)
    ]
    fp_yn = [
        remote("fp_yn", fp.at[EDGES + 96 * k:EDGES + 96 * (k + 1)], fy.at[96 * k:96 * (k + 1)], y_peer, k, 2)
        for k in range(2)
    ]
    def fp_after_x(k):
        fp_x[k].wait_recv()
        add_into(fs.at[chunk(k, 128)], fp[chunk(2 * h + k, 128)], fx[chunk(k, 128)])
        pl.when(s == 0)(fp_y[k].start)

    g2_compute(1)
    g2_compute(2)
    for k in range(2):
        rows = chunk(2 * (1 - h) + k, 128)
        fp[rows] = nt(dxw[rows], ww[...]).astype(BF)
        fp_x[k].start()
    g2_after_twin(1)
    g2_after_twin(2)
    fp[EDGES:TOTAL] = nt(dxw[EDGES:TOTAL], ww[...]).astype(BF)

    @pl.when(s == 1)
    def _():
        for copy in fp_yn:
            copy.start()

    fp[pl.ds(own, 256)] = nt(dxw[pl.ds(own, 256)], ww[...]).astype(BF)
    fp_after_x(0)
    fp_after_x(1)

    @pl.when(s == 0)
    def _():
        for k in range(2):
            fp_yn[k].wait_recv()
            at = slice(256 + 96 * k, 256 + 96 * (k + 1))
            add_into(fs.at[at], fp[EDGES + 96 * k:EDGES + 96 * (k + 1)], fy[96 * k:96 * (k + 1)])
            pl.when(h == 1)(fp_xn[k].start)

    qkv_bias_sum = col_sum(dxw[...].astype(F32))

    g1_after_y(2)
    st1[0] = g1_after_z(0)

    def first_rows(rows, fg):
        n1, r1 = normed(res[rows].astype(F32))
        g = fg * a_gain
        back = r1 * (
            g - jnp.mean(g, axis=-1, keepdims=True) - n1 * jnp.mean(g * n1, axis=-1, keepdims=True)
        )
        dtv[rows] = (mgd[rows] + back).astype(BF)
        return jnp.concatenate([col_sum(fg * n1), col_sum(fg)], axis=0)

    def own_chunk(k, n):
        return pl.ds(pl.multiple_of(own + n * k, n), n)

    dt_e = [
        remote("dt", dtv.at[128 * k:128 * (k + 1)], d_tok.at[own_chunk(k, 128)], x_peer, k, 2)
        for k in range(2)
    ]
    dt_n = remote("dt", dtv.at[0:NODES], d_tok.at[0:NODES], x_peer, 0, 2)
    va[...] = jnp.zeros_like(va)

    @pl.when(s == 1)
    def _():
        for k in range(2):
            fp_y[k].wait_recv()

            def edge_rows(i, carry):
                rows = pl.ds(pl.multiple_of(128 * k + 64 * i, 64), 64)
                return carry + first_rows(rows, fs[rows].astype(F32) + fy[rows].astype(F32))

            got = lax.fori_loop(0, 2, edge_rows, jnp.zeros((2, 768), F32))
            va[0:2] += got
            dt_e[k].start()

    @pl.when((s == 0) & (h == 0))
    def _():
        for k in range(2):
            fp_xn[k].wait_recv()

            def node_rows(i, carry):
                rows = pl.ds(pl.multiple_of(96 * k + 32 * i, 32), 32)
                from_fs = pl.ds(pl.multiple_of(256 + 96 * k + 32 * i, 32), 32)
                return carry + first_rows(rows, fs[from_fs].astype(F32) + fx[from_fs].astype(F32))

            got = lax.fori_loop(0, 3, node_rows, jnp.zeros((2, 768), F32))
            va[0:2] += got
        dtv[NODES:256] = mgd[NODES:256].astype(BF)
        dt_n.start()

    @pl.when((s == 0) & (h == 1))
    def _():
        dtv[...] = mgd[...].astype(BF)

    stores[1].start()

    sums = [f_gain_sum, f_shift_sum, out_bias_sum, down_bias_sum, up_bias_sum, va[0:1], va[1:2], zero_row]
    sums += [jnp.where(me == r, qkv_bias_sum, 0.0) for r in range(4)] + [zero_row] * 4
    vq[me] = jnp.concatenate(sums, axis=0)
    v1 = [remote("v_q", vq.at[me], vq.at[me], dev, k, 3) for k, dev in enumerate(quad)]
    for copy in v1:
        copy.start()

    st1[1] = g1_after_z(1)
    st2[1] = g2_after_z(1)
    st2[2] = g2_after_z(2)
    f1_after_z(0, st1[0])
    f2_after_z(0, st2[0])
    st1[2] = g1_after_z(2)
    v1_in = [
        remote("v_q", vq.at[r], vq.at[r], dev, k, 3)
        for k, (dev, r) in enumerate(zip(quad, (2 * s + 1 - h, 2 - 2 * s + h, 3 - 2 * s - h)))
    ]
    for copy in v1_in:
        copy.wait_recv()
    vz[z] = vq[0] + vq[1] + vq[2] + vq[3]
    v2 = [remote("v_z", vz.at[z], vz.at[z], z_peers[d], d, zc - 1) for d in range(zc - 1)]
    for copy in v2:
        copy.start()
    f1_after_z(1, st1[1])
    f2_after_z(1, st2[1])
    f2_after_z(2, st2[2])
    f1_after_y(0)
    f2_after_y(0)
    for copy in v2:
        copy.wait_recv()
    vsum = vz[0]
    for d in range(1, zc):
        vsum = vsum + vz[d]
    vc[c] = vsum
    v3 = remote("v_c", vc.at[c], vc.at[c], twin)
    v3.start()
    f1_after_z(2, st1[2])
    f1_after_y(1)
    f2_after_y(1)
    f2_after_y(2)
    f1_after_y(2)
    v3.wait_recv()
    vec[...] = vc[0] + vc[1]
    for copy in (*f1_c, *f2_c):
        copy.wait_recv()
    for copy in stores[0:2]:
        copy.wait()

    @pl.when(s == 1)
    def _():
        for copy in (*dt_e, out_send):
            copy.wait()

    @pl.when(me == 0)
    def _():
        for copy in (dt_n, out_node):
            copy.wait_send()
        for copy in far:
            copy.wait()

    @pl.when(me == 1)
    def _():
        for copy in (dt_n, out_node):
            copy.wait_recv()
        for copy in near:
            copy.wait()

    @pl.when(s == 1)
    def _():
        for copy in tok_y:
            copy.wait_send()

    @pl.when(s == 0)
    def _():
        tok_n.wait_send()
        for copy in tok_x:
            copy.wait_send()

    wait_sent("att", att, ain)

    @pl.when(s == 0)
    def _():
        for copy in fp_y:
            copy.wait_send()

    @pl.when(me == 1)
    def _():
        for copy in fp_xn:
            copy.wait_send()

    @pl.when(s == 1)
    def _():
        for copy in fp_yn:
            copy.wait_send()

    @pl.when(s == 1)
    def _():
        w_out[0].wait_send()
        w_out[2].wait_send()
        w_y[0].wait_send()
        w_y[2].wait_send()

    for k, (dev_sh, first, count) in enumerate(OWNERS):
        mine = 2 * dev_sh[0] + dev_sh[1]

        @pl.when(me == mine)
        def _():
            for r in range(4):
                if r != mine:
                    i = sem_id("da_s", 4) + r
                    pltpu.make_async_remote_copy(
                        src_ref=ago.at[0:count, 0:256], dst_ref=da.at[first:first + count],
                        send_sem=ss.at[i], recv_sem=rs.at[i], device_id=x_peer, device_id_type=MESH,
                    ).wait_send()

    for copy in (
        u_send, w_out[1], *w_twin, *g1_twin, *g1_x, *g1_y, *sum(g1_z, []), *fp_x, *g2_twin,
        *sum(g2_z, []), *v1, *sum(f1_z, []), *f1_y, *f1_c, *sum(f2_z, []), *f2_y, *f2_c, *v2, v3,
    ):
        copy.wait_send()


def finish_kernel(
    tokens, cot, d_out, d_tok, f1, f2, vec,
    output, tokens_grad, a_gain, a_shift, wq, bq, wk, wv, bv, wo, bo, f_gain, f_shift, wu, bu, wd, bd,
):
    h = lax.axis_index("head")
    output[...] = tokens[...].astype(F32) + d_out[...].astype(F32)
    tokens_grad[...] = cot[...] + d_tok[...].astype(F32)
    for k in range(2):
        lanes = slice(384 * k, 384 * (k + 1))
        wd[:, lanes] = f1[0, k].astype(F32)
        wo[:, lanes] = f1[2, k].astype(F32)
        wu[k] = f1[1, k].astype(F32)
    low_half = lax.broadcasted_iota(jnp.int32, (1, 128), 1) < 64
    tile = lambda k, t: f2[k, :, 128 * t:128 * (t + 1)].astype(F32)
    for t, out in ((0, wv), (2, wq), (3, wk)):
        out[:, 0:128] = tile(0, t)
        out[:, 256:384] = tile(1, t)
    wq[:, 128:256] = jnp.where(low_half, tile(0, 4), tile(1, 4))
    wk[:, 128:256] = pltpu.roll(jnp.where(low_half, tile(1, 4), tile(0, 4)), 64, 1)
    wv[:, 128:256] = jnp.where(low_half, tile(0, 1), tile(1, 1))

    @pl.when(pl.program_id(0) == 0)
    def _():
        mine = pl.ds(pl.multiple_of(384 * h, 384), 384)
        for row, out in ((0, f_gain), (1, f_shift), (2, bo), (3, bd), (4, bu), (5, a_gain), (6, a_shift)):
            out[...] = vec[row:row + 1, mine].reshape(384)
        low = jnp.where(h == 0, vec[8:9], vec[9:10])
        high = jnp.where(h == 0, vec[10:11], vec[11:12])
        for first, out in ((0, bq), (512, bv)):
            a, b = low[:, first:first + 256], high[:, first:first + 256]
            parts = [a[:, 0:128], a[:, 128:256] + b[:, 0:128], b[:, 128:256]]
            out[...] = jnp.concatenate(parts, axis=1).reshape(384)


def fast_layer(
    tokens, cotangent, attn_gain, attn_shift, query_weight, query_bias, key_weight, value_weight,
    value_bias, out_weight, out_bias, ffn_gain, ffn_shift, up_weight, up_bias, down_weight,
    down_bias, atom_counts, edge_counts,
):
    zc = lax.axis_size("mol") // 2
    anywhere = pl.BlockSpec(memory_space=pl.ANY)
    vmem = pl.BlockSpec(memory_space=pltpu.VMEM)
    smem = pl.BlockSpec(memory_space=pltpu.SMEM)
    shape = jax.ShapeDtypeStruct
    SEM.clear()
    buf = lambda dtype, *dims: pltpu.VMEM(dims, dtype)
    scratch = [
        buf(BF, 256, 768), buf(BF, 256, 768), buf(BF, 256, 768), buf(BF, 3, 192 // zc, 384), buf(BF, 384 // zc, 640), buf(BF, TOTAL, 640),
        buf(BF, PADDED, 768), buf(BF, 256, 768), buf(F32, 256, 768), buf(BF, 768, 768),
        buf(BF, 2, 384, 768), buf(BF, 2, 768, 384), buf(BF, 2, 384, 768), buf(F32, 2, 8, 384),
        buf(BF, PADDED, 768), buf(BF, PADDED, 768), buf(BF, TOTAL, 768),
        buf(BF, HEADS_HERE, TOTAL, 256), buf(BF, HEADS_HERE, TOTAL, 256),
        buf(BF, 1024, 512), buf(BF, 1024, 512), buf(BF, 1024, 512), buf(BF, 1024, 512), buf(BF, 1536, 768),
        buf(F32, 256, 768), buf(jnp.int32, TOTAL, 1),
        buf(F32, TOTAL, 256), buf(BF, TOTAL, 256), buf(BF, 4, 256, 256), buf(BF, TOTAL, 256), buf(F32, TOTAL, 128),
        buf(F32, 256, 768), buf(F32, 256, 768), buf(F32, 256, 768), buf(F32, 256, 128), buf(F32, 256, 768),
        buf(BF, 256, 768), buf(BF, 256, 768), buf(BF, 256, 768), buf(BF, 256, 768), buf(BF, 256, 768),
        buf(BF, 256, 768), buf(BF, 256, 768), buf(F32, 256, 768),
        buf(BF, 1536, 768), buf(F32, PADDED, 256), buf(F32, PADDED, 256),
        buf(BF, 3, 2, 2, 384, 384), buf(BF, 3, 2, 384, 384), buf(BF, 3, 384, 384), buf(BF, 3, 2, 384, 384),
        buf(BF, 3, 2, 192, 384), buf(BF, 3, 192, 384), buf(BF, 3, zc - 1, 192 // zc, 384),
        buf(BF, 2, 384, 640), buf(BF, 384, 640), buf(BF, zc - 1, 384 // zc, 640),
        buf(BF, TOTAL, 768), buf(BF, 256 + NODES, 768), buf(BF, 256 + NODES, 768), buf(BF, 256, 768),
        buf(F32, 8, 768), buf(F32, 4, 16, 768), buf(F32, zc, 16, 768), buf(F32, 2, 16, 768),
        pltpu.SemaphoreType.DMA((N_SEMS,)), pltpu.SemaphoreType.DMA((N_SEMS,)), pltpu.SemaphoreType.DMA((N_LOCAL,)),
    ]
    d_out, d_tok, f1, f2, vec = pl.pallas_call(
        layer_kernel,
        out_shape=[
            shape((512, 768), BF), shape((512, 768), BF), shape((3, 2, 384, 384), BF),
            shape((2, 768, 640), BF), shape((16, 768), F32),
        ],
        in_specs=[anywhere] * 8 + [smem] * 2 + [vmem] * 9,
        out_specs=[anywhere] * 4 + [vmem],
        scratch_shapes=scratch,
        compiler_params=pltpu.CompilerParams(
            collective_id=0, has_side_effects=True, vmem_limit_bytes=61 * 2**20
        ),
        name="layer",
    )(
        tokens, cotangent, query_weight, key_weight, value_weight, out_weight, up_weight, down_weight,
        atom_counts, edge_counts, attn_gain, attn_shift, query_bias, value_bias, out_bias,
        ffn_gain, ffn_shift, up_bias, down_bias,
    )
    assert sum(n for _, n in SEM.values()) <= N_SEMS
    steps = 4
    mat, tall, line = shape((384, 768), F32), shape((768, 384), F32), shape((384,), F32)
    big, pair = shape((512, 768), F32), shape((2, 384, 384), F32)
    by_rows = lambda rows, cols: pl.BlockSpec((rows // steps, cols), lambda i: (i, 0))
    big_spec, mat_spec, tall_spec = by_rows(512, 768), by_rows(384, 768), by_rows(768, 384)
    line_spec = pl.BlockSpec((384,), lambda i: (0,))
    pair_spec = pl.BlockSpec((2, 384 // steps, 384), lambda i: (0, i, 0))
    outs = pl.pallas_call(
        finish_kernel,
        grid=(steps,),
        out_shape=[big, big, line, line, tall, line, tall, tall, line, mat, line, line, line, pair, line, mat, line],
        in_specs=[
            big_spec, big_spec, big_spec, big_spec,
            pl.BlockSpec((3, 2, 384 // steps, 384), lambda i: (0, 0, i, 0)),
            pl.BlockSpec((2, 768 // steps, 640), lambda i: (0, i, 0)),
            pl.BlockSpec((16, 768), lambda i: (0, 0)),
        ],
        out_specs=[
            big_spec, big_spec, line_spec, line_spec, tall_spec, line_spec, tall_spec, tall_spec, line_spec,
            mat_spec, line_spec, line_spec, line_spec, pair_spec, line_spec, mat_spec, line_spec,
        ],
        compiler_params=pltpu.CompilerParams(vmem_limit_bytes=60 * 2**20),
        name="finish",
    )(tokens, cotangent, d_out, d_tok, f1, f2, vec)
    return tuple(o.reshape(768, 384) if o.ndim == 3 else o for o in outs)


def plain_dot(operand, partner):
    return jnp.dot(operand, partner, preferred_element_type=jnp.float32)


def lead_dot(operand, partner):
    return lax.dot_general(
        operand, partner, (((0,), (0,)), ((), ())), preferred_element_type=jnp.float32
    )


def tail_dot(operand, partner):
    return lax.dot_general(
        operand, partner, (((1,), (1,)), ((), ())), preferred_element_type=jnp.float32
    )


def norm_apply(values, gain_vec, shift_vec):
    row_mean = jnp.mean(values, axis=-1, keepdims=True)
    centered = values - row_mean
    variance = jnp.mean(centered * centered, axis=-1, keepdims=True)
    return centered * lax.rsqrt(variance + 1e-05) * gain_vec + shift_vec


def gelu_exact(values):
    return jax.nn.gelu(values, approximate=False)


def segment_ids(counts, added, slot_count):
    members = jnp.arange(counts.shape[0])
    earlier = members[:, None] <= members[None, :]
    seg_ends = jnp.sum(jnp.where(earlier, (counts + added)[:, None], 0), axis=0)
    positions = jnp.arange(slot_count, dtype=jnp.int32)
    return jnp.sum((positions[:, None] >= seg_ends[None, :]).astype(jnp.int32), axis=1)


def head_piece(vector, head_rank, head_share):
    return lax.dynamic_slice_in_dim(vector, head_rank * head_share, head_share)


def on_device(
    tokens,
    cotangent,
    attn_gain,
    attn_shift,
    query_weight,
    query_bias,
    key_weight,
    value_weight,
    value_bias,
    out_weight,
    out_bias,
    ffn_gain,
    ffn_shift,
    up_weight,
    up_bias,
    down_weight,
    down_bias,
    atom_counts,
    edge_counts,
):
    row_count = tokens.shape[0]
    model_width = tokens.shape[1]
    local_width = query_weight.shape[1]
    local_heads = local_width // HEAD_DIM
    head_count = lax.axis_size("head")
    head_rank = lax.axis_index("head")
    stream_rank = lax.axis_index("stream")
    molecules = atom_counts.shape[1]
    head_share = model_width // head_count
    score_scale = HEAD_DIM ** (-0.5)
    seg_node = segment_ids(atom_counts[0], 1, row_count)
    seg_edge = segment_ids(edge_counts[0], 0, row_count)
    key_seg = jnp.concatenate([seg_node, seg_edge])
    own_seg = jnp.where(stream_rank == 0, seg_node, seg_edge)
    live_rows = (own_seg < molecules).astype(jnp.float32)[:, None]
    residual = tokens.astype(jnp.float32)
    normed, norm_pull = jax.vjp(norm_apply, residual, attn_gain, attn_shift)
    first_in = normed.astype(jnp.bfloat16)
    queries = (plain_dot(first_in, query_weight) + query_bias).astype(jnp.bfloat16)
    keys_local = plain_dot(first_in, key_weight).astype(jnp.bfloat16)
    values_local = (plain_dot(first_in, value_weight) + value_bias).astype(jnp.bfloat16)
    all_keys, all_values = (
        lax.all_gather(keys_local, "stream", axis=0, tiled=True),
        lax.all_gather(values_local, "stream", axis=0, tiled=True),
    )
    key_count = all_keys.shape[0]
    key_heads = all_keys.reshape(key_count, local_heads, HEAD_DIM)
    value_heads = all_values.reshape(key_count, local_heads, HEAD_DIM)
    blocks = row_count // 512
    block_rows = row_count // blocks
    query_blocks = queries.reshape(blocks, block_rows, local_heads, HEAD_DIM)
    seg_blocks = own_seg.reshape(blocks, block_rows)

    def forward_block(pieces):
        query_part, seg_part = pieces
        scores = (
            jnp.einsum("qhd,khd->hqk", query_part, key_heads, preferred_element_type=jnp.float32)
            * score_scale
        )
        same_mol = (seg_part[:, None] == key_seg[None, :])[None]
        scores = jnp.where(same_mol, scores, -1e30)
        row_top = jnp.max(scores, axis=-1, keepdims=True)
        shifted = jnp.exp(scores - row_top)
        row_total = jnp.sum(shifted, axis=-1, keepdims=True)
        prob_low = (shifted / row_total).astype(jnp.bfloat16)
        attended_part = jnp.einsum(
            "hqk,khd->qhd", prob_low, value_heads, preferred_element_type=jnp.float32
        )
        return (attended_part.astype(jnp.bfloat16), (row_top + jnp.log(row_total))[..., 0])

    attended_blocks, lse_blocks = lax.map(forward_block, (query_blocks, seg_blocks))
    attended = attended_blocks.reshape(row_count, local_width)
    attn_sum = lax.psum(plain_dot(attended, out_weight), "head")
    middle = residual + live_rows * (attn_sum + out_bias)
    second, second_pull = jax.vjp(norm_apply, middle, ffn_gain, ffn_shift)
    second_in = second.astype(jnp.bfloat16)
    inner_pre = plain_dot(second_in, up_weight) + up_bias.astype(jnp.float32)
    activated, gelu_pull = jax.vjp(gelu_exact, inner_pre)
    hidden = activated.astype(jnp.bfloat16)
    ffn_sum = lax.psum(plain_dot(hidden, down_weight).astype(jnp.bfloat16), "head").astype(
        jnp.float32
    )
    output = middle + live_rows * (ffn_sum + down_bias)
    down_cot = (live_rows * cotangent).astype(jnp.bfloat16)
    down_weight_grad = lead_dot(hidden, down_cot)
    down_bias_full = jnp.sum(down_cot.astype(jnp.float32), axis=0)
    inner_grad = gelu_pull(tail_dot(down_cot, down_weight))[0].astype(jnp.bfloat16)
    up_weight_grad = lead_dot(second_in, inner_grad)
    up_bias_grad = jnp.sum(inner_grad.astype(jnp.float32), axis=0)
    second_grad = lax.psum(tail_dot(inner_grad, up_weight), "head")
    middle_part, ffn_gain_full, ffn_shift_full = second_pull(second_grad)
    mid_grad = cotangent + middle_part
    ffn_gain_grad = head_piece(ffn_gain_full, head_rank, head_share)
    ffn_shift_grad = head_piece(ffn_shift_full, head_rank, head_share)
    down_bias_grad = head_piece(down_bias_full, head_rank, head_share)
    attn_cot = (live_rows * mid_grad).astype(jnp.bfloat16)
    out_weight_grad = lead_dot(attended, attn_cot)
    out_bias_full = jnp.sum(attn_cot.astype(jnp.float32), axis=0)
    attended_grad = tail_dot(attn_cot, out_weight).astype(jnp.bfloat16)
    grad_blocks = attended_grad.reshape(blocks, block_rows, local_heads, HEAD_DIM)

    def backward_block(running, pieces):
        key_acc, value_acc = running
        query_part, seg_part, lse_part, grad_part = pieces
        scores = (
            jnp.einsum("qhd,khd->hqk", query_part, key_heads, preferred_element_type=jnp.float32)
            * score_scale
        )
        same_mol = (seg_part[:, None] == key_seg[None, :])[None]
        prob_full = jnp.where(same_mol, jnp.exp(scores - lse_part[..., None]), 0.0)
        prob_low = prob_full.astype(jnp.bfloat16)
        prob_grad = jnp.einsum(
            "qhd,khd->hqk", grad_part, value_heads, preferred_element_type=jnp.float32
        )
        row_delta = jnp.sum(prob_grad * prob_full, axis=-1, keepdims=True)
        score_grad = (prob_full * (prob_grad - row_delta)).astype(jnp.bfloat16)
        query_part_grad = (
            jnp.einsum("hqk,khd->qhd", score_grad, key_heads, preferred_element_type=jnp.float32)
            * score_scale
        )
        key_acc = (
            key_acc
            + jnp.einsum("hqk,qhd->khd", score_grad, query_part, preferred_element_type=jnp.float32)
            * score_scale
        )
        value_acc = value_acc + jnp.einsum(
            "hqk,qhd->khd", prob_low, grad_part, preferred_element_type=jnp.float32
        )
        return ((key_acc, value_acc), query_part_grad.astype(jnp.bfloat16))

    zero_keys = jnp.zeros((key_count, local_heads, HEAD_DIM), jnp.float32)
    (key_acc, value_acc), query_grads = lax.scan(
        backward_block, (zero_keys, zero_keys), (query_blocks, seg_blocks, lse_blocks, grad_blocks)
    )
    key_sum, value_sum = (
        lax.psum_scatter(
            key_acc.reshape(key_count, local_width), "stream", scatter_dimension=0, tiled=True
        ),
        lax.psum_scatter(
            value_acc.reshape(key_count, local_width), "stream", scatter_dimension=0, tiled=True
        ),
    )
    key_grad = key_sum.astype(jnp.bfloat16)
    value_grad = value_sum.astype(jnp.bfloat16)
    query_grad = query_grads.reshape(row_count, local_width)
    query_weight_grad = lead_dot(first_in, query_grad)
    query_bias_grad = jnp.sum(query_grad.astype(jnp.float32), axis=0)
    key_weight_grad = lead_dot(first_in, key_grad)
    value_weight_grad = lead_dot(first_in, value_grad)
    value_bias_grad = jnp.sum(value_grad.astype(jnp.float32), axis=0)
    first_part = (
        tail_dot(query_grad, query_weight)
        + tail_dot(key_grad, key_weight)
        + tail_dot(value_grad, value_weight)
    )
    first_grad = lax.psum(first_part.astype(jnp.bfloat16), "head").astype(jnp.float32)
    resid_part, attn_gain_full, attn_shift_full = norm_pull(first_grad)
    tokens_grad = mid_grad + resid_part
    attn_gain_grad = head_piece(attn_gain_full, head_rank, head_share)
    attn_shift_grad = head_piece(attn_shift_full, head_rank, head_share)
    out_bias_grad = head_piece(out_bias_full, head_rank, head_share)
    (
        attn_gain_grad,
        attn_shift_grad,
        query_weight_grad,
        query_bias_grad,
        key_weight_grad,
        value_weight_grad,
        value_bias_grad,
        out_weight_grad,
        out_bias_grad,
        ffn_gain_grad,
        ffn_shift_grad,
        up_weight_grad,
        up_bias_grad,
        down_weight_grad,
        down_bias_grad,
    ) = lax.psum(
        (
            attn_gain_grad,
            attn_shift_grad,
            query_weight_grad,
            query_bias_grad,
            key_weight_grad,
            value_weight_grad,
            value_bias_grad,
            out_weight_grad,
            out_bias_grad,
            ffn_gain_grad,
            ffn_shift_grad,
            up_weight_grad,
            up_bias_grad,
            down_weight_grad,
            down_bias_grad,
        ),
        ("mol", "stream"),
    )
    return (
        output,
        tokens_grad,
        attn_gain_grad,
        attn_shift_grad,
        query_weight_grad,
        query_bias_grad,
        key_weight_grad,
        value_weight_grad,
        value_bias_grad,
        out_weight_grad,
        out_bias_grad,
        ffn_gain_grad,
        ffn_shift_grad,
        up_weight_grad,
        up_bias_grad,
        down_weight_grad,
        down_bias_grad,
    )


def solution(mesh):
    in_specs = (
        P(("mol", "stream"), None),
        P(("mol", "stream"), None),
        P(),
        P(),
        P(None, "head"),
        P("head"),
        P(None, "head"),
        P(None, "head"),
        P("head"),
        P("head", None),
        P(),
        P(),
        P(),
        P(None, "head"),
        P("head"),
        P("head", None),
        P(),
        P("mol", None),
        P("mol", None),
    )
    out_specs = (
        P(("mol", "stream"), None),
        P(("mol", "stream"), None),
        P("head"),
        P("head"),
        P(None, "head"),
        P("head"),
        P(None, "head"),
        P(None, "head"),
        P("head"),
        P("head", None),
        P("head"),
        P("head"),
        P("head"),
        P(None, "head"),
        P("head"),
        P("head", None),
        P("head"),
    )
    one_chip_pair = (
        mesh.shape["head"] == 2 and mesh.shape["stream"] == 2 and mesh.shape["mol"] == 8
    )
    return jax.shard_map(
        fast_layer if one_chip_pair else on_device, mesh=mesh, in_specs=in_specs, out_specs=out_specs, check_vma=False
    )
```

profile of v0, /device:TPU:0, one launch (start us, length us, event | category | flops | bytes accessed | tf_op | source)
XLA Modules:
  0.0 127.1 jit_solution(5899615255074928414)
XLA Ops:
  0.7 118.9 %layer.1 = (bf16[512,768]{1,0:T(8,128)(2,1)}, bf16[512,768]{1,0:T(8,128)(2,1)}, bf16[3,2,384,384]{3,2,1,0:T(8,128)(2,1)}, bf16[2,768,640]{2,1,0:T(8,128)(2,1)}, f32[16,768]{1,0:T(8,128)}) custom-call(bf16[512,768]{1,0:T(8,128)(2,1)} %tokens.3, f32[512,768]{1,0:T(8,128)} %cot.3, bf16[768,384]{1,0:T(8,128)(2,1)} %wq.1, bf16[768,384]{1,0:T(8,128)(2,1)} %wk.1, ...), custom_call_target="tpu_custom_call" | custom-call | tf_op jit(solution)/shard_map/layer/pallas_call | solution.py:1077
  119.5 7.4 %finish.1 = (f32[512,768]{1,0:T(8,128)}, f32[512,768]{1,0:T(8,128)}, f32[384]{0:T(512)}, f32[384]{0:T(512)}, f32[768,384]{1,0:T(8,128)}, /*index=5*/f32[384]{0:T...) custom-call(bf16[512,768]{1,0:T(8,128)(2,1)} %tokens.3, ...), custom_call_target="tpu_custom_call" | custom-call | tf_op jit(solution)/shard_map/finish/pallas_call | solution.py:1103
where the time goes:
time: 128 us; the launch traced here: 127 us
  Pallas kernels  126 us (98%)
    pallas_call x1, Pallas kernels, fast_layer(): pl.pallas_call(layer_kernel, out_shape=[shape((512, 768), BF), shape((512...  119 us
    pallas_call x1, Pallas kernels, fast_layer(): pl.pallas_call(finish_kernel, grid=(steps,), out_shape=[big, big, line, l...  7.38 us

commit v1 on v0

--- a/solution.py
+++ b/solution.py
@@ -82,7 +82,7 @@
     p0, p1, p2, p3, p4, bias, segc, attf, att, ain, da, delta,
     t0, t1, n2s, r2s, mid, sec, hid, dc, ig, ac, ato, ago, mgd,
     ds, dkf, dvf,
-    g1, gs1, xr, gx, yr, gq, zr1, g2, gs2, zr2, fp, fx, fs, fy,
+    g1, gs1, qr, xr, gx, yr, gq, zr1, g2, gs2, zr2, fp, fx, fs, fy,
     va, vq, vz, vc,
     ss, rs, ls,
 ):
@@ -403,7 +403,12 @@
 
     rows_y = pl.ds(pl.multiple_of(192 * (1 - s), 192), 192)
     rows_s = pl.ds(pl.multiple_of(192 * s, 192), 192)
-    y_first = (True, True, False)
+    y_first = (None, True, False)
+    g1_q = [
+        remote("g1_q", gs1.at[0, 1 - h, rows_s], qr.at[0], x_peer, 0, 3),
+        remote("g1_q", gs1.at[0, h, rows_y], qr.at[1], y_peer, 1, 3),
+        remote("g1_q", gs1.at[0, 1 - h, rows_y], qr.at[2], xy_peer, 2, 3),
+    ]
     g1_x = [
         remote("g1_x", gx.at[p, 1 - h, 0:192], xr.at[p, 0:192], x_peer, p, 3)
         if y_first[p] else remote("g1_x", gs1.at[p, 1 - h], xr.at[p], x_peer, p, 3)
@@ -438,7 +443,13 @@
         g1_twin[p].wait_recv()
         for xh in range(2):
             add_into(gs1.at[p, xh], g1[p, c, xh], gs1[p, xh])
-        (g1_y if y_first[p] else g1_x)[p].start()
+
+    def g1_after_quad():
+        for copy in g1_q:
+            copy.wait_recv()
+        add_into(gq.at[0], gs1[0, h, rows_s], qr[0], qr[1], qr[2])
+        for copy in g1_z[0]:
+            copy.start()
 
     def g1_after_x(p):
         g1_x[p].wait_recv()
@@ -526,8 +537,6 @@
     other_rows = pl.ds(other, 256)
     out_send = remote("out", dov, d_out.at[own_rows], x_peer)
     out_node = remote("out", dov.at[0:NODES], d_out.at[0:NODES], x_peer)
-    pl.when(s == 1)(out_send.start)
-    pl.when(me == 0)(out_node.start)
     g1_compute(0)
     stores = [local(10, dov, d_out.at[own_rows])]
     stores[0].start()
@@ -553,7 +562,6 @@
         return carry + col_sum(x.astype(F32))
 
     up_bias_sum = row_loop(256, 64, inner_rows, zero_row)
-    g1_after_twin(0)
     t0[...] = nt(ig[:, 0:384], fwu[0]) + nt(ig[:, 384:768], fwu[1])
 
     def second_rows(rows, carry):
@@ -592,8 +600,8 @@
 
     g1_compute(1)
     g1_compute(2)
-    g1_after_twin(1)
-    g1_after_twin(2)
+    for p in range(3):
+        g1_after_twin(p)
 
     for k, (dev_sh, first, count) in enumerate(OWNERS):
         mine = 2 * dev_sh[0] + dev_sh[1]
@@ -606,6 +614,8 @@
                 send_sem=ss.at[j], recv_sem=rs.at[j], device_id=x_peer, device_id_type=MESH,
             ).wait_recv()
 
+    for copy in (*g1_q, g1_y[1], g1_x[2]):
+        copy.start()
     head_col = lax.broadcasted_iota(jnp.int32, (256, 128), 1)
     lane_row = lax.broadcasted_iota(jnp.int32, (256, 128), 0) - 64 * s
     head_pick = jnp.where(
@@ -735,7 +745,7 @@
 
     dxp[:, 0:128], dxp[:, 128:256] = tiles_of(2)
     g2_compute(0)
-    g1_after_y(0)
+    g1_after_quad()
     for b, (q0, qn, segs) in enumerate(BLOCKS):
         pr = probs[b]
         for j0 in range(0, HEADS_HERE, group):
@@ -768,11 +778,12 @@
         if b == 0:
             g2_after_twin(0)
         if b == 1:
-            g1_after_x(0)
             g1_after_y(1)
         if b == 2:
             g1_after_x(2)
         if b == 3:
+            st1[0] = g1_after_z(0)
+        if b == 4:
             g1_after_x(1)
             st2[0] = g2_after_z(0)
     dxw[:, 256:512] = (dkf[0:TOTAL] * SCALE).astype(BF)
@@ -817,8 +828,14 @@
             copy.start()
 
     fp[pl.ds(own, 256)] = nt(dxw[pl.ds(own, 256)], ww[...]).astype(BF)
+    g1_after_y(2)
     fp_after_x(0)
+    st1[1] = g1_after_z(1)
     fp_after_x(1)
+    pl.when(s == 1)(out_send.start)
+    pl.when(me == 0)(out_node.start)
+    f1_after_z(0, st1[0])
+    f2_after_z(0, st2[0])
 
     @pl.when(s == 0)
     def _():
@@ -830,8 +847,8 @@
 
     qkv_bias_sum = col_sum(dxw[...].astype(F32))
 
-    g1_after_y(2)
-    st1[0] = g1_after_z(0)
+    st2[1] = g2_after_z(1)
+    st2[2] = g2_after_z(2)
 
     def first_rows(rows, fg):
         n1, r1 = normed(res[rows].astype(F32))
@@ -893,12 +910,9 @@
     for copy in v1:
         copy.start()
 
-    st1[1] = g1_after_z(1)
-    st2[1] = g2_after_z(1)
-    st2[2] = g2_after_z(2)
-    f1_after_z(0, st1[0])
-    f2_after_z(0, st2[0])
     st1[2] = g1_after_z(2)
+    f1_after_z(1, st1[1])
+    f1_after_y(0)
     v1_in = [
         remote("v_q", vq.at[r], vq.at[r], dev, k, 3)
         for k, (dev, r) in enumerate(zip(quad, (2 * s + 1 - h, 2 - 2 * s + h, 3 - 2 * s - h)))
@@ -909,11 +923,11 @@
     v2 = [remote("v_z", vz.at[z], vz.at[z], z_peers[d], d, zc - 1) for d in range(zc - 1)]
     for copy in v2:
         copy.start()
-    f1_after_z(1, st1[1])
     f2_after_z(1, st2[1])
     f2_after_z(2, st2[2])
-    f1_after_y(0)
+    f1_after_z(2, st1[2])
     f2_after_y(0)
+    f1_after_y(1)
     for copy in v2:
         copy.wait_recv()
     vsum = vz[0]
@@ -922,8 +936,6 @@
     vc[c] = vsum
     v3 = remote("v_c", vc.at[c], vc.at[c], twin)
     v3.start()
-    f1_after_z(2, st1[2])
-    f1_after_y(1)
     f2_after_y(1)
     f2_after_y(2)
     f1_after_y(2)
@@ -1002,7 +1014,7 @@
                     ).wait_send()
 
     for copy in (
-        u_send, w_out[1], *w_twin, *g1_twin, *g1_x, *g1_y, *sum(g1_z, []), *fp_x, *g2_twin,
+        u_send, w_out[1], *w_twin, *g1_twin, *g1_q, *g1_x[1:], *g1_y[1:], *sum(g1_z, []), *fp_x, *g2_twin,
         *sum(g2_z, []), *v1, *sum(f1_z, []), *f1_y, *f1_c, *sum(f2_z, []), *f2_y, *f2_c, *v2, v3,
     ):
         copy.wait_send()
@@ -1067,7 +1079,7 @@
         buf(BF, 256, 768), buf(BF, 256, 768), buf(BF, 256, 768), buf(BF, 256, 768), buf(BF, 256, 768),
         buf(BF, 256, 768), buf(BF, 256, 768), buf(F32, 256, 768),
         buf(BF, 1536, 768), buf(F32, PADDED, 256), buf(F32, PADDED, 256),
-        buf(BF, 3, 2, 2, 384, 384), buf(BF, 3, 2, 384, 384), buf(BF, 3, 384, 384), buf(BF, 3, 2, 384, 384),
+        buf(BF, 3, 2, 2, 384, 384), buf(BF, 3, 2, 384, 384), buf(BF, 3, 192, 384), buf(BF, 3, 384, 384), buf(BF, 3, 2, 384, 384),
         buf(BF, 3, 2, 192, 384), buf(BF, 3, 192, 384), buf(BF, 3, zc - 1, 192 // zc, 384),
         buf(BF, 2, 384, 640), buf(BF, 384, 640), buf(BF, zc - 1, 384 // zc, 640),
         buf(BF, TOTAL, 768), buf(BF, 256 + NODES, 768), buf(BF, 256 + NODES, 768), buf(BF, 256, 768),

time: 128 us -> 122 us (0.953)
  Pallas kernels: 126 us -> 121 us
    pallas_call x1, Pallas kernels: 119 us -> 114 us  [fast_layer(): pl.pallas_call(layer_kernel, out_shape=[shape((512, 768), BF), shape((512...]
where the time goes in v1:
time: 122 us
  Pallas kernels  121 us (99%)
    pallas_call x1, Pallas kernels, fast_layer(): pl.pallas_call(layer_kernel, out_shape=[shape((512, 768), BF), shape((512...  114 us
    pallas_call x1, Pallas kernels, fast_layer(): pl.pallas_call(finish_kernel, grid=(steps,), out_shape=[big, big, line, l...  7.38 us

profile of v1, /device:TPU:0, one launch (start us, length us, event | category | flops | bytes accessed | tf_op | source)
XLA Modules:
  0.0 122.2 jit_solution(14795863632806894982)
XLA Ops:
  0.7 114.0 %layer.1 = (bf16[512,768]{1,0:T(8,128)(2,1)}, bf16[512,768]{1,0:T(8,128)(2,1)}, bf16[3,2,384,384]{3,2,1,0:T(8,128)(2,1)}, bf16[2,768,640]{2,1,0:T(8,128)(2,1)}, f32[16,768]{1,0:T(8,128)}) custom-call(bf16[512,768]{1,0:T(8,128)(2,1)} %tokens.3, f32[512,768]{1,0:T(8,128)} %cot.3, bf16[768,384]{1,0:T(8,128)(2,1)} %wq.1, bf16[768,384]{1,0:T(8,128)(2,1)} %wk.1, ...), custom_call_target="tpu_custom_call" | custom-call | tf_op jit(solution)/shard_map/layer/pallas_call | solution.py:1089
  114.7 7.4 %finish.1 = (f32[512,768]{1,0:T(8,128)}, f32[512,768]{1,0:T(8,128)}, f32[384]{0:T(512)}, f32[384]{0:T(512)}, f32[768,384]{1,0:T(8,128)}, /*index=5*/f32[384]{0:T...) custom-call(bf16[512,768]{1,0:T(8,128)(2,1)} %tokens.3, ...), custom_call_target="tpu_custom_call" | custom-call | tf_op jit(solution)/shard_map/finish/pallas_call | solution.py:1115

commit v2 on v1

--- a/solution.py
+++ b/solution.py
@@ -242,6 +242,12 @@
         ],
         axis=1,
     )
+
+    for who, slot in ((0, qr.at[0]), (3, qr.at[1]), (2, qr.at[2]), (3, yr.at[1, 0]), (3, yr.at[1, 1]), (0, xr.at[2])):
+
+        @pl.when(me == who)
+        def _():
+            slot[...] = jnp.zeros_like(slot)
 
     def project(first, count):
         def norm_rows(i, carry):
@@ -445,14 +451,17 @@
             add_into(gs1.at[p, xh], g1[p, c, xh], gs1[p, xh])
 
     def g1_after_quad():
-        for copy in g1_q:
-            copy.wait_recv()
+        for copy, without in zip(g1_q, (0, 3, 2)):
+            pl.when(me != without)(copy.wait_recv)
         add_into(gq.at[0], gs1[0, h, rows_s], qr[0], qr[1], qr[2])
         for copy in g1_z[0]:
             copy.start()
 
     def g1_after_x(p):
-        g1_x[p].wait_recv()
+        if y_first[p]:
+            g1_x[p].wait_recv()
+        else:
+            pl.when(me != 0)(g1_x[p].wait_recv)
         if y_first[p]:
             add_into(gq.at[p], gx[p, h, 0:192], xr[p, 0:192])
             for copy in g1_z[p]:
@@ -462,7 +471,10 @@
             g1_y[p].start()
 
     def g1_after_y(p):
-        g1_y[p].wait_recv()
+        if y_first[p]:
+            pl.when(me != 3)(g1_y[p].wait_recv)
+        else:
+            g1_y[p].wait_recv()
         if y_first[p]:
             for xh in range(2):
                 add_into(gx.at[p, xh, 0:192], gs1[p, xh, rows_s], yr[p, xh])
@@ -614,8 +626,11 @@
                 send_sem=ss.at[j], recv_sem=rs.at[j], device_id=x_peer, device_id_type=MESH,
             ).wait_recv()
 
-    for copy in (*g1_q, g1_y[1], g1_x[2]):
-        copy.start()
+    @pl.when(me != 1)
+    def _():
+        for copy in (*g1_q, g1_y[1], g1_x[2]):
+            copy.start()
+
     head_col = lax.broadcasted_iota(jnp.int32, (256, 128), 1)
     lane_row = lax.broadcasted_iota(jnp.int32, (256, 128), 0) - 64 * s
     head_pick = jnp.where(
@@ -786,6 +801,7 @@
         if b == 4:
             g1_after_x(1)
             st2[0] = g2_after_z(0)
+    g1_after_y(2)
     dxw[:, 256:512] = (dkf[0:TOTAL] * SCALE).astype(BF)
     q_full, q_half = tiles_of(0)
     k_full, k_half = tiles_of(1)
@@ -828,13 +844,12 @@
             copy.start()
 
     fp[pl.ds(own, 256)] = nt(dxw[pl.ds(own, 256)], ww[...]).astype(BF)
-    g1_after_y(2)
+    st1[1] = g1_after_z(1)
+    f1_after_z(0, st1[0])
     fp_after_x(0)
-    st1[1] = g1_after_z(1)
     fp_after_x(1)
     pl.when(s == 1)(out_send.start)
     pl.when(me == 0)(out_node.start)
-    f1_after_z(0, st1[0])
     f2_after_z(0, st2[0])
 
     @pl.when(s == 0)
@@ -911,8 +926,11 @@
         copy.start()
 
     st1[2] = g1_after_z(2)
+    f2_after_z(1, st2[1])
+    f2_after_z(2, st2[2])
     f1_after_z(1, st1[1])
     f1_after_y(0)
+    f2_after_y(0)
     v1_in = [
         remote("v_q", vq.at[r], vq.at[r], dev, k, 3)
         for k, (dev, r) in enumerate(zip(quad, (2 * s + 1 - h, 2 - 2 * s + h, 3 - 2 * s - h)))
@@ -923,11 +941,10 @@
     v2 = [remote("v_z", vz.at[z], vz.at[z], z_peers[d], d, zc - 1) for d in range(zc - 1)]
     for copy in v2:
         copy.start()
-    f2_after_z(1, st2[1])
-    f2_after_z(2, st2[2])
     f1_after_z(2, st1[2])
-    f2_after_y(0)
     f1_after_y(1)
+    f2_after_y(1)
+    f2_after_y(2)
     for copy in v2:
         copy.wait_recv()
     vsum = vz[0]
@@ -936,8 +953,6 @@
     vc[c] = vsum
     v3 = remote("v_c", vc.at[c], vc.at[c], twin)
     v3.start()
-    f2_after_y(1)
-    f2_after_y(2)
     f1_after_y(2)
     v3.wait_recv()
     vec[...] = vc[0] + vc[1]
@@ -974,6 +989,11 @@
     def _():
         tok_n.wait_send()
         for copy in tok_x:
+            copy.wait_send()
+
+    @pl.when(me != 1)
+    def _():
+        for copy in (*g1_q, g1_y[1], g1_x[2]):
             copy.wait_send()
 
     wait_sent("att", att, ain)
@@ -1014,7 +1034,7 @@
                     ).wait_send()
 
     for copy in (
-        u_send, w_out[1], *w_twin, *g1_twin, *g1_q, *g1_x[1:], *g1_y[1:], *sum(g1_z, []), *fp_x, *g2_twin,
+        u_send, w_out[1], *w_twin, *g1_twin, g1_x[1], g1_y[2], *sum(g1_z, []), *fp_x, *g2_twin,
         *sum(g2_z, []), *v1, *sum(f1_z, []), *f1_y, *f1_c, *sum(f2_z, []), *f2_y, *f2_c, *v2, v3,
     ):
         copy.wait_send()

time: 122 us -> 121 us (level); the launches traced: 122 us -> 119 us
  Pallas kernels: 121 us -> 119 us
    pallas_call x1, Pallas kernels: 114 us -> 111 us  [fast_layer(): pl.pallas_call(layer_kernel, out_shape=[shape((512, 768), BF), shape((512...]
where the time goes in v2:
time: 121 us; the launch traced here: 119 us
  Pallas kernels  119 us (98%)
    pallas_call x1, Pallas kernels, fast_layer(): pl.pallas_call(layer_kernel, out_shape=[shape((512, 768), BF), shape((512...  111 us
    pallas_call x1, Pallas kernels, fast_layer(): pl.pallas_call(finish_kernel, grid=(steps,), out_shape=[big, big, line, l...  7.38 us

profile of v2, /device:TPU:0, one launch (start us, length us, event | category | flops | bytes accessed | tf_op | source)
XLA Modules:
  0.0 119.4 jit_solution(3174920957856801186)
XLA Ops:
  0.7 111.2 %layer.1 = (bf16[512,768]{1,0:T(8,128)(2,1)}, bf16[512,768]{1,0:T(8,128)(2,1)}, bf16[3,2,384,384]{3,2,1,0:T(8,128)(2,1)}, bf16[2,768,640]{2,1,0:T(8,128)(2,1)}, f32[16,768]{1,0:T(8,128)}) custom-call(bf16[512,768]{1,0:T(8,128)(2,1)} %tokens.3, f32[512,768]{1,0:T(8,128)} %cot.3, bf16[768,384]{1,0:T(8,128)(2,1)} %wq.1, bf16[768,384]{1,0:T(8,128)(2,1)} %wk.1, ...), custom_call_target="tpu_custom_call" | custom-call | tf_op jit(solution)/shard_map/layer/pallas_call | solution.py:1109
  111.9 7.4 %finish.1 = (f32[512,768]{1,0:T(8,128)}, f32[512,768]{1,0:T(8,128)}, f32[384]{0:T(512)}, f32[384]{0:T(512)}, f32[768,384]{1,0:T(8,128)}, /*index=5*/f32[384]{0:T...) custom-call(bf16[512,768]{1,0:T(8,128)(2,1)} %tokens.3, ...), custom_call_target="tpu_custom_call" | custom-call | tf_op jit(solution)/shard_map/finish/pallas_call | solution.py:1135

commit v3 on v2

--- a/solution.py
+++ b/solution.py
@@ -1125,7 +1125,7 @@
         ffn_gain, ffn_shift, up_bias, down_bias,
     )
     assert sum(n for _, n in SEM.values()) <= N_SEMS
-    steps = 4
+    steps = 2
     mat, tall, line = shape((384, 768), F32), shape((768, 384), F32), shape((384,), F32)
     big, pair = shape((512, 768), F32), shape((2, 384, 384), F32)
     by_rows = lambda rows, cols: pl.BlockSpec((rows // steps, cols), lambda i: (i, 0))

time: 121 us -> 120 us (level)
  no operation moved by 1% of the time
where the time goes in v3:
time: 120 us; the launch traced here: 119 us
  Pallas kernels  118 us (98%)
    pallas_call x1, Pallas kernels, fast_layer(): pl.pallas_call(layer_kernel, out_shape=[shape((512, 768), BF), shape((512...  111 us
    pallas_call x1, Pallas kernels, fast_layer(): pl.pallas_call(finish_kernel, grid=(steps,), out_shape=[big, big, line, l...  6.47 us

profile of v3, /device:TPU:0, one launch (start us, length us, event | category | flops | bytes accessed | tf_op | source)
XLA Modules:
  0.0 118.5 jit_solution(14129319952422363838)
XLA Ops:
  0.7 111.2 %layer.1 = (bf16[512,768]{1,0:T(8,128)(2,1)}, bf16[512,768]{1,0:T(8,128)(2,1)}, bf16[3,2,384,384]{3,2,1,0:T(8,128)(2,1)}, bf16[2,768,640]{2,1,0:T(8,128)(2,1)}, f32[16,768]{1,0:T(8,128)}) custom-call(bf16[512,768]{1,0:T(8,128)(2,1)} %tokens.3, f32[512,768]{1,0:T(8,128)} %cot.3, bf16[768,384]{1,0:T(8,128)(2,1)} %wq.1, bf16[768,384]{1,0:T(8,128)(2,1)} %wk.1, ...), custom_call_target="tpu_custom_call" | custom-call | tf_op jit(solution)/shard_map/layer/pallas_call | solution.py:1109
  111.9 6.5 %finish.1 = (f32[512,768]{1,0:T(8,128)}, f32[512,768]{1,0:T(8,128)}, f32[384]{0:T(512)}, f32[384]{0:T(512)}, f32[768,384]{1,0:T(8,128)}, /*index=5*/f32[384]{0:T...) custom-call(bf16[512,768]{1,0:T(8,128)(2,1)} %tokens.3, ...), custom_call_target="tpu_custom_call" | custom-call | tf_op jit(solution)/shard_map/finish/pallas_call | solution.py:1135
